TPU v7x, 256 devices: a whole 4x4x8 slice. The times are simulated.
256 devices in a mesh: dp: 16 (over x, y_lo, core), shard: 16 (over z, y_hi).
Axes of the slice: x: 4, y: 4 (y_hi: 2, y_lo: 2; y = y_hi * 2 + y_lo), z: 8, core: 2. Of those that a mesh axis runs over, the one named last changes fastest.
Arguments:
- hidden: bfloat16 [2048, 16384], P('dp', 'shard'), may hold values from -6 to 6
- head_weight: bfloat16 [16384, 16384], P('shard', 'dp'), may hold values from -0.046875 to 0.046875
- vocab_head: bfloat16 [16384, 4096], P('shard'), may hold values from -0.0546875 to 0.0546875
- targets: int32 [2048], P('dp'), may hold values from 0 to 4095
Outputs:
- grad_weight: bfloat16 [16384, 16384], P('dp', 'shard')
- token_loss: float32 [2048], P('dp')
All inputs are finite; a program needn't handle non-finite values.
Results may differ from a plain program's by a relative error of at most 0.014.
Values may be sent and summed in bfloat16 or wider, within the bound.
A program may use at most 128 MiB of HBM per device.

v0:
```python
import jax
import jax.numpy as jnp
from jax import lax
from jax.sharding import PartitionSpec as P


def body(hidden, head_weight, vocab_head, targets):
    dp_size = lax.axis_size("dp")
    shard_size = lax.axis_size("shard")
    rows = hidden.shape[0]
    feats = hidden.shape[1]
    units = head_weight.shape[1]
    sub_rows = rows // shard_size
    per_group = dp_size * sub_rows
    all_hidden = lax.all_gather(hidden, "dp", axis=0, tiled=True)
    grouped = all_hidden.reshape(dp_size, shard_size, sub_rows, feats)
    term = lax.dot_general(
        grouped, head_weight, (((3,), (0,)), ((), ())), preferred_element_type=jnp.float32
    )
    middle = lax.psum_scatter(
        jnp.transpose(term, (1, 0, 2, 3))
        .reshape(per_group * lax.axis_size("shard"), units)
        .astype(jnp.bfloat16),
        "shard",
        scatter_dimension=0,
        tiled=True,
    ).astype(jnp.float32)
    pre = lax.all_to_all(
        lax.all_to_all(middle.astype(jnp.bfloat16), "dp", split_axis=0, concat_axis=1, tiled=True),
        "shard",
        split_axis=1,
        concat_axis=0,
        tiled=True,
    ).astype(middle.dtype)
    resout = (hidden.astype(jnp.float32) + jax.nn.silu(pre)).astype(jnp.bfloat16)
    partial_logits = jnp.dot(resout, vocab_head, preferred_element_type=jnp.float32)
    vocab_size = vocab_head.shape[1]
    logits = lax.psum(partial_logits.astype(jnp.bfloat16), "shard").astype(jnp.float32)
    positions = lax.broadcasted_iota(jnp.int32, (rows, vocab_size), 1)
    onehot = (positions == targets[:, None]).astype(jnp.float32)
    expo = jnp.exp(logits)
    total = jnp.sum(expo, axis=1)
    picked = jnp.sum(onehot * logits, axis=1)
    token_loss = jnp.log(total) - picked
    grads = (expo / total[:, None] - onehot).astype(jnp.bfloat16)
    dres = lax.dot_general(
        grads, vocab_head, (((1,), (1,)), ((), ())), preferred_element_type=jnp.float32
    )
    sig = jax.nn.sigmoid(pre)
    dpre = (dres * (sig * (1.0 + pre * (1.0 - sig)))).astype(jnp.bfloat16)
    full_units = lax.all_gather(dpre, "shard", axis=1, tiled=True)
    columns = lax.all_to_all(full_units, "dp", split_axis=1, concat_axis=0, tiled=True)
    grad = lax.dot_general(
        columns, all_hidden, (((0,), (0,)), ((), ())), preferred_element_type=jnp.float32
    )
    return (grad.astype(jnp.bfloat16), token_loss)


def solution(mesh):
    in_specs = (P("dp", "shard"), P("shard", "dp"), P("shard", None), P("dp"))
    out_specs = (P("dp", "shard"), P("dp"))
    return jax.shard_map(body, mesh=mesh, in_specs=in_specs, out_specs=out_specs, check_vma=False)
```

profile of v0, /device:TPU:32, one launch (start us, length us, event | category | flops | bytes accessed | tf_op | source)
XLA Modules:
  0.0 650.8 jit_solution(6920729305752435221)
XLA Ops:
  7.2 0.0 copy-start
  7.2 0.0 all-gather.3.cloned.1.call-start
  7.2 0.7 all-gather.3.cloned.1.call-update
  7.9 0.0 reduce-scatter.2.cloned.1.call-start
  8.0 44.4 %all-gather.3.cloned.1.call-done = bf16[2048,1024]{1,0:T(8,128)(2,1)} async-done(((bf16[128,1024]{1,0:T(8,128)(2,1)}), bf16[2048,1024]{1,0:T(8,128)(2,1)}) %all-gather.3.cloned.1.call-update) | async-done | bytes 4194320 | tf_op jit(solution)/shard_map/all_gather | solution.py:15
  52.4 0.0 copy-done
  52.4 6.9 %convert_bitcast_fusion = bf16[16,16,8,1024]{3,2,0,1:T(8,128)(2,1)S(1)} fusion(bf16[16,16,8,1024]{3,2,1,0:T(8,128)(2,1)} %bitcast.55, bf16[1024,1024]{1,0:T(8,128)(2,1)S(1)} %copy-done), kind=kOutput, calls=%fused_computation.2 | convolution fusion | flops 4297064448 | bytes 10485760 | tf_op jit(solution)/shard_map/dot_general | solution.py:17
  59.3 2.4 copy.6
  61.7 0.0 copy-start.1
  61.7 0.0 reduce-scatter.2.cloned.1.call-update
  61.8 0.0 all-reduce.2.cloned.1.call-start
  61.8 211.4 %reduce-scatter.2.cloned.1.call-done = bf16[128,1024]{1,0:T(8,128)(2,1)} async-done(((bf16[2048,1024]{1,0:T(8,128)(2,1)}), bf16[128,1024]{1,0:T(8,128)(2,1)}) %reduce-scatter.2.cloned.1.call-update) | async-done | bytes 262160 | tf_op jit(solution)/shard_map/reduce_scatter | solution.py:20
  273.3 12.0 %all_to_all.45 = bf16[16,8,1024]{2,1,0:T(8,128)(2,1)S(1)} all-to-all(bf16[16,8,1024]{2,1,0:T(8,128)(2,1)} %bitcast.54), channel_id=1, replica_groups=mesh['dp'=16,'shard'=16] {'dp'}, dimensions={0} | all-to-all | bytes 524288 | tf_op jit(solution)/shard_map/all_to_all | solution.py:29
  285.3 20.6 %all_to_all.46 = bf16[8,16,1024]{2,0,1:T(8,128)(2,1)S(1)} all-to-all(bf16[8,16,1024]{2,0,1:T(8,128)(2,1)S(1)} %bitcast.53), channel_id=1, replica_groups=mesh['dp'=16,'shard'=16] {'shard'}, dimensions={1} | all-to-all | bytes 524288 | tf_op jit(solution)/shard_map/all_to_all | solution.py:28
  305.9 0.0 copy-done.1
  305.9 0.0 copy-start.2
  305.9 5.7 convolution_convert_fusion
  311.6 0.0 all-reduce.2.cloned.1.call-update
  311.6 0.0 all-gather.5.cloned.1.call-start
  311.7 154.0 %all-reduce.2.cloned.1.call-done = bf16[128,4096]{1,0:T(8,128)(2,1)} async-done(((bf16[128,4096]{1,0:T(8,128)(2,1)}), bf16[128,4096]{1,0:T(8,128)(2,1)}) %all-reduce.2.cloned.1.call-update) | async-done | bytes 1048592 | tf_op jit(solution)/shard_map/psum | solution.py:38
  465.6 0.0 copy-done.2
  465.6 1.9 fusion.4
  467.6 7.4 %fusion.6 = bf16[128,1024]{1,0:T(8,128)(2,1)} fusion(bf16[1024,4096]{1,0:T(8,128)(2,1)} %param.6, bf16[128,4096]{1,0:T(8,128)(2,1)} %all-reduce.2.cloned.1.call-done, s32[128]{0:T(128)S(1)} %copy-done.2, f32[128]{0:T(128)S(1)} %get-tuple-element.3, bf16[8,16,1024]{2,0,1:T(8,128)(2,1)S(1)} %all_to_all.46), kind=kOutput, calls=%fused_computation.14 | convolution fusion | flops 1078198272 | bytes 9962496 | tf_op jit(solution)/shard_map/dot_general | solution.py:46
  474.9 0.0 all-gather.5.cloned.1.call-update
  475.0 98.3 %all-gather.5.cloned.1.call-done = bf16[128,16384]{1,0:T(8,128)(2,1)} async-done(((bf16[128,1024]{1,0:T(8,128)(2,1)}), bf16[128,16384]{1,0:T(8,128)(2,1)}) %all-gather.5.cloned.1.call-update) | async-done | bytes 4194320 | tf_op jit(solution)/shard_map/all_gather | solution.py:51
  573.3 4.8 copy.11
  578.1 4.7 all-to-all-start.2
  582.8 0.5 log_subtract_fusion
  583.4 51.5 %all-to-all-done.2 = bf16[128,16,1024]{2,0,1:T(8,128)(2,1)} async-done(((bf16[128,16,1024]{2,0,1:T(8,128)(2,1)}), bf16[128,16,1024]{2,0,1:T(8,128)(2,1)}, u32[]{:S(2)}, u32[]{:S(2)}) %all-to-all-start.2) | async-done | bytes 4194336 | tf_op jit(solution)/shard_map/all_to_all | solution.py:52
  634.9 9.4 %convolution_convert_fusion.1 = bf16[1024,1024]{1,0:T(8,128)(2,1)} fusion(bf16[2048,1024]{1,0:T(8,128)(2,1)} %bitcast.11, bf16[2048,1024]{1,0:T(8,128)(2,1)} %all-gather.3.cloned.1.call-done), kind=kOutput, calls=%fused_computation.12 | convolution fusion | flops 4296015872 | bytes 10485760 | tf_op jit(solution)/shard_map/dot_general | solution.py:53
Async XLA Ops:
  7.2 45.2 %copy-start = (bf16[1024,1024]{1,0:T(8,128)(2,1)S(1)}, bf16[1024,1024]{1,0:T(8,128)(2,1)}, u32[]{:S(2)}) copy-start(bf16[1024,1024]{1,0:T(8,128)(2,1)} %param.5) | copy-start | bytes 6291460
  7.2 45.2 %all-gather.3.cloned.1.call-start = ((), (), s32[]{:S(2)}) async-start(), calls=%async_computation.4 | async-start | bytes 4456448 | tf_op jit(solution)/shard_map/all_gather | solution.py:15
  7.9 265.3 %reduce-scatter.2.cloned.1.call-start = ((), (), s32[]{:S(2)}) async-start(), calls=%async_computation.5 | async-start | bytes 4456448 | tf_op jit(solution)/shard_map/reduce_scatter | solution.py:20
  61.7 244.2 %copy-start.1 = (bf16[128,1024]{1,0:T(8,128)(2,1)S(1)}, bf16[128,1024]{1,0:T(8,128)(2,1)}, u32[]{:S(2)}) copy-start(bf16[128,1024]{1,0:T(8,128)(2,1)} %param.4) | copy-start | bytes 786436
  61.8 403.9 %all-reduce.2.cloned.1.call-start = ((), (), s32[]{:S(2)}) async-start(), calls=%async_computation.6 | async-start | bytes 2097152 | tf_op jit(solution)/shard_map/psum | solution.py:38
  305.9 159.7 %copy-start.2 = (s32[128]{0:T(128)S(1)}, s32[128]{0:T(128)}, u32[]{:S(2)}) copy-start(s32[128]{0:T(128)} %param.7) | copy-start | bytes 1540
  311.6 261.7 %all-gather.5.cloned.1.call-start = ((), (), s32[]{:S(2)}) async-start(), calls=%async_computation.7 | async-start | bytes 4456448 | tf_op jit(solution)/shard_map/all_gather | solution.py:51
  578.1 56.8 %all-to-all-start.2 = ((bf16[128,16,1024]{2,0,1:T(8,128)(2,1)}), bf16[128,16,1024]{2,0,1:T(8,128)(2,1)}, u32[]{:S(2)}, u32[]{:S(2)}) async-start(bf16[128,16,1024]{2,0,1:T(8,128)(2,1)} %bitcast.51), calls=%async_computation.3 | async-start | bytes 8388608 | tf_op jit(solution)/shard_map/all_to_all | solution.py:52
Sparse Core Ops, SparseCore 0:
  9.9 42.4 all-gather.2
  61.9 211.3 reduce-scatter.1
  311.7 153.8 all-reduce.1
  475.1 98.1 all-gather.4
where the time goes:
time: 658 us; the launch traced here: 651 us
  waiting for transfers between devices  560 us (85%)
  blocking collectives  32.6 us (5%)
  matrix products  29.3 us (4%)
  between operations  13.8 us (2%)
  local copies, waits for them, and re-layouts  7.26 us (1%)
    reduce_scatter x1, waiting for transfers between devices, body(): lax.psum_scatter(jnp.transpose(term, (1, 0, 2, 3)).reshape(per_group * la...  211 us
    psum x1, waiting for transfers between devices, body(): lax.psum(partial_logits.astype(jnp.bfloat16), 'shard').astype(jnp.float32)  154 us
    all_gather x1, waiting for transfers between devices, body(): full_units = lax.all_gather(dpre, 'shard', axis=1, tiled=True)  98.3 us
    all_to_all x1, waiting for transfers between devices, body(): lax.all_to_all(full_units, 'dp', split_axis=1, concat_axis=0, tiled=True)  51.5 us
    all_gather x1, waiting for transfers between devices, body(): all_hidden = lax.all_gather(hidden, 'dp', axis=0, tiled=True)  44.4 us
    all_to_all x1, blocking collectives, body(): lax.all_to_all(lax.all_to_all(middle.astype(jnp.bfloat16), 'dp', split_ax...  20.6 us
  transfers between devices with their start and end apart: 5, of which 5 were waited for; matrix products, arithmetic and copies ran while one was open for 0% of the time, Pallas kernels for 0%

commit v1 on v0

v1 whole, which is shorter than its diff:
```python
import jax
import jax.numpy as jnp
from jax import lax
from jax.experimental import pallas as pl
from jax.experimental.pallas import tpu as pltpu
from jax.sharding import PartitionSpec as P

MESH = pl.DeviceIdType.MESH
BF16 = jnp.bfloat16
F32 = jnp.float32

ROUNDS = 8
RING = 8
PARTS = 4


def slot_of(dx, a):
    odd = dx % 2
    return odd * (2 + 2 * a + (3 - dx) // 2) + (1 - odd) * (3 * dx + a)


def offset_of(slot):
    middle = jnp.logical_and(slot >= 2, slot <= 5)
    dx = jnp.where(middle, 3 - 2 * (slot % 2), jnp.where(slot >= 6, 2, 0))
    a = jnp.where(middle, (slot // 2 + 1) % 2, slot % 2)
    return dx, a


def send(src, dst, send_sem, recv_sem, device):
    pltpu.make_async_remote_copy(
        src_ref=src,
        dst_ref=dst,
        send_sem=send_sem,
        recv_sem=recv_sem,
        device_id=device,
        device_id_type=MESH,
    ).start()


def wait(ref, sem):
    pltpu.make_async_copy(ref, ref, sem).wait()


def kernel(
    h_in, w_in, v_in, tgt, out, loss_out,
    H, W, V, PT, S0, R, YS, YK, YR, TS, PRE, RES, D1, L, SL, RL, LYS, LYR, LF, G, DR, DQ, DP, ACC, OUT,
    loc, h_sib, h_far, h_r, rs_s, rs_r, y_s, y_r, t_s, t_r, l_s, l_r, ly_s, ly_r, g_s, g_r,
    d_s, d_r, dy_s, dy_r, a_s, a_r, o_s,
):
    dp = lax.axis_index("dp")
    shard = lax.axis_index("shard")
    x, y_lo, core = dp // 4, (dp // 2) % 2, dp % 2
    z, y_hi = shard // 2, shard % 2
    feats = H.shape[3]
    units = W.shape[1]
    vq = L.shape[3]
    voc = vq * PARTS

    x_next = ((dp + 4) % 16, shard)
    x_prev = ((dp + 12) % 16, shard)
    y_near = (dp + 2 - 4 * y_lo, shard)
    sibling = (dp + 1 - 2 * core, shard)
    z_next = (dp, (shard + 2) % 16)
    z_prev = (dp, (shard + 14) % 16)
    y_far = (dp, shard + 1 - 2 * y_hi)
    ring = (z_next, z_prev)

    def out_target(slot):
        dx, a = offset_of(slot)
        there = ((x + dx) % 4) * 4 + ((y_lo + a) % 2) * 2 + (core + shard // 8) % 2
        return (there, dp)

    flip = (core + shard % 2) % 2

    def in_source(g):
        return (shard, 8 * flip + g)

    def is_self(device):
        return jnp.logical_and(device[0] == dp, device[1] == shard)

    barrier = pltpu.get_barrier_semaphore()
    for device in (x_next, x_prev, y_near, sibling, z_next, z_prev, y_far):
        pl.semaphore_signal(barrier, inc=1, device_id=device, device_id_type=MESH)
    for n in range(8):
        for device in (out_target(jnp.int32(n)), in_source(n)):
            @pl.when(jnp.logical_not(is_self(device)))
            def _(device=device):
                pl.semaphore_signal(barrier, inc=1, device_id=device, device_id_type=MESH)
    own = jnp.logical_and(dp == shard, dp < 8)
    copy_w = pltpu.make_async_copy(w_in, W, loc.at[0])
    copy_w.start()
    copy_v = pltpu.make_async_copy(v_in, V, loc.at[1])
    copy_h = pltpu.make_async_copy(h_in, H.at[0, 0], loc.at[2])
    copy_h.start()
    pl.semaphore_wait(barrier, jnp.where(own, 21, 23))

    send(h_in, H.at[0, 1], h_sib.at[0], h_r.at[0, 1], sibling)
    send(h_in, H.at[1, 0], h_far.at[0], h_r.at[1, 0], y_near)
    send(h_in, H.at[2, 0], h_far.at[1], h_r.at[2, 0], x_next)
    send(h_in, H.at[3, 0], h_far.at[2], h_r.at[3, 0], x_prev)
    copy_v.start()

    def service(q):
        wait(H.at[q, 0], h_r.at[q, 0])
        send(H.at[q, 0], H.at[q, 1], h_sib.at[q], h_r.at[q, 1], sibling)

        @pl.when(q == 1)
        def _():
            send(H.at[1, 0], H.at[4, 0], h_far.at[3], h_r.at[4, 0], x_next)
            send(H.at[1, 0], H.at[5, 0], h_far.at[4], h_r.at[5, 0], x_prev)

        @pl.when(q == 2)
        def _():
            send(H.at[2, 0], H.at[6, 0], h_far.at[5], h_r.at[6, 0], x_next)

        @pl.when(q == 5)
        def _():
            send(H.at[5, 0], H.at[7, 0], h_far.at[6], h_r.at[7, 0], x_prev)

    copy_h.wait()
    copy_w.wait()

    def ahead(d, k):
        return (z + (RING // 2 - k if d == 0 else RING // 2 + k)) % RING

    nt = min(512, units)

    def product(t):
        def tile(n, _):
            cols = pl.ds(pl.multiple_of(n * nt, nt), nt)
            rows = H[t].reshape(256, feats)
            PT[t, :, :, cols] = jnp.dot(
                rows, W[:, cols], preferred_element_type=F32
            ).reshape(RING, 32, nt)
            return 0

        lax.fori_loop(0, units // nt, tile, 0)

    def live(r, n):
        return jnp.logical_and(r >= 0, r < n)

    def pre_tick(t, _):
        r5 = t - 5

        @pl.when(live(r5, ROUNDS))
        def _():
            wait(YR.at[r5], y_r.at[r5])
            TS[r5] = (YK[r5] + YR[r5].astype(F32)).astype(BF16)
            device = out_target(r5)
            g = shard % 8

            @pl.when(is_self(device))
            def _():
                pltpu.make_async_copy(TS.at[r5], PRE.at[g], t_r.at[g]).start()

            @pl.when(jnp.logical_not(is_self(device)))
            def _():
                send(TS.at[r5], PRE.at[g], t_s.at[r5], t_r.at[g], device)

        r4 = t - 4

        @pl.when(live(r4, ROUNDS))
        def _():
            wait(R.at[0, r4, 3], rs_r.at[0, r4, 3])
            wait(R.at[1, r4, 3], rs_r.at[1, r4, 3])
            mine = pl.ds(pl.multiple_of(y_hi * 16, 16), 16)
            other = pl.ds(pl.multiple_of(16 - y_hi * 16, 16), 16)
            YS[r4] = (
                PT[r4, z, other] + R[0, r4, 3, other].astype(F32) + R[1, r4, 3, other].astype(F32)
            ).astype(BF16)
            send(YS.at[r4], YR.at[r4], y_s.at[r4], y_r.at[r4], y_far)
            YK[r4] = PT[r4, z, mine] + R[0, r4, 3, mine].astype(F32) + R[1, r4, 3, mine].astype(F32)

        for k in (3, 2, 1):
            rk = t - k

            @pl.when(live(rk, ROUNDS))
            def _(k=k, rk=rk):
                for d in (0, 1):
                    at = ahead(d, k)
                    if k == 1:
                        half = slice(d * 16, d * 16 + 16)
                        rest = slice(16 - d * 16, 32 - d * 16)
                        wait(R.at[d, rk, 0, half], rs_r.at[d, rk, 0])
                        R[d, rk, 0, half] = (
                            PT[rk, at, half] + R[d, rk, 0, half].astype(F32)
                        ).astype(BF16)
                        R[d, rk, 0, rest] = PT[rk, at, rest].astype(BF16)
                    else:
                        wait(R.at[d, rk, k - 1], rs_r.at[d, rk, k - 1])
                        R[d, rk, k - 1] = (
                            PT[rk, at] + R[d, rk, k - 1].astype(F32)
                        ).astype(BF16)
                    send(R.at[d, rk, k - 1], R.at[d, rk, k], rs_s.at[d, rk, k], rs_r.at[d, rk, k], ring[d])

        @pl.when(t == 1)
        def _():
            service(t)

        @pl.when(t < ROUNDS)
        def _():
            wait(H.at[t, 1], h_r.at[t, 1])
            product(t)
            for d in (0, 1):
                half = slice(d * 16, d * 16 + 16)
                S0[d, t] = PT[t, ahead(d, 0), half].astype(BF16)
                send(S0.at[d, t], R.at[d, t, 0, half], rs_s.at[d, t, 0], rs_r.at[d, t, 0], ring[d])

        @pl.when(jnp.logical_and(t >= 1, t < ROUNDS - 1))
        def _():
            service(t + 1)

        return 0

    lax.fori_loop(0, ROUNDS + 5, pre_tick, 0)

    for g in range(8):
        wait(PRE.at[g], t_r.at[g])
    pre = PRE[...].reshape(128, units).astype(F32)
    RES[...] = (H[0, 0].astype(F32) + pre / (1.0 + jnp.exp(-pre))).astype(BF16)
    copy_v.wait()

    hc = vq // 2

    def logit_tick(t, _):
        p5 = t - 5

        @pl.when(live(p5, PARTS))
        def _():
            wait(LYR.at[p5], ly_r.at[p5])
            LF[p5] = LYS[p5].astype(F32) + LYR[p5].astype(F32)

        p4 = t - 4

        @pl.when(live(p4, PARTS))
        def _():
            wait(RL.at[0, p4, 3], l_r.at[0, p4, 3])
            wait(RL.at[1, p4, 3], l_r.at[1, p4, 3])
            LYS[p4] = (
                L[p4, z] + RL[0, p4, 3].astype(F32) + RL[1, p4, 3].astype(F32)
            ).astype(BF16)
            send(LYS.at[p4], LYR.at[p4], ly_s.at[p4], ly_r.at[p4], y_far)

        for k in (3, 2, 1):
            pk = t - k

            @pl.when(live(pk, PARTS))
            def _(k=k, pk=pk):
                for d in (0, 1):
                    at = ahead(d, k)
                    if k == 1:
                        half = slice(d * hc, d * hc + hc)
                        rest = slice(hc - d * hc, 2 * hc - d * hc)
                        wait(RL.at[d, pk, 0, :, half], l_r.at[d, pk, 0])
                        RL[d, pk, 0, :, half] = (
                            L[pk, at, :, half] + RL[d, pk, 0, :, half].astype(F32)
                        ).astype(BF16)
                        RL[d, pk, 0, :, rest] = L[pk, at, :, rest].astype(BF16)
                    else:
                        wait(RL.at[d, pk, k - 1], l_r.at[d, pk, k - 1])
                        RL[d, pk, k - 1] = (
                            L[pk, at] + RL[d, pk, k - 1].astype(F32)
                        ).astype(BF16)
                    send(RL.at[d, pk, k - 1], RL.at[d, pk, k], l_s.at[d, pk, k], l_r.at[d, pk, k], ring[d])

        @pl.when(t < PARTS)
        def _():
            cols = pl.ds(pl.multiple_of(t * vq, vq), vq)
            L[t] = jnp.dot(RES[...], V[:, cols], preferred_element_type=F32).reshape(RING, 16, vq)
            for d in (0, 1):
                half = slice(d * hc, d * hc + hc)
                SL[d, t] = L[t, ahead(d, 0), :, half].astype(BF16)
                send(SL.at[d, t], RL.at[d, t, 0, :, half], l_s.at[d, t, 0], l_r.at[d, t, 0], ring[d])

        return 0

    lax.fori_loop(0, PARTS + 5, logit_tick, 0)

    total = jnp.zeros((16, 1), F32)
    picked = jnp.zeros((16, 1), F32)
    target = tgt[z]
    for p in range(PARTS):
        logits = LF[p]
        hit = lax.broadcasted_iota(jnp.int32, (16, vq), 1) + p * vq == target
        total += jnp.sum(jnp.exp(logits), axis=1, keepdims=True)
        picked += jnp.sum(jnp.where(hit, logits, 0.0), axis=1, keepdims=True)
    for p in range(PARTS):
        hit = lax.broadcasted_iota(jnp.int32, (16, vq), 1) + p * vq == target
        G[z, :, p * vq:(p + 1) * vq] = (
            jnp.exp(LF[p]) / total - jnp.where(hit, 1.0, 0.0)
        ).astype(BF16)
    loss = jnp.log(total) - picked
    high = loss.astype(BF16).astype(F32)
    middle = (loss - high).astype(BF16).astype(F32)
    low = loss - high - middle
    lane = lax.broadcasted_iota(jnp.int32, (16, 128), 1)
    G[z, :, voc:] = jnp.where(
        lane == 0, high, jnp.where(lane == 1, middle, jnp.where(lane == 2, low, 0.0))
    ).astype(BF16)

    spans = ((0, voc // 4, voc // 2), (voc // 2, 3 * voc // 4, voc + 128))

    def behind(d, k):
        return (z + (RING - k if d == 0 else k)) % RING

    def span(p, d):
        return slice(spans[p][d], spans[p][d + 1])

    def grad_step(p, k):
        for d in (0, 1):
            every = slice(spans[p][0], spans[p][2])
            here = behind(d, k)
            if k > 0:
                got = span(p, d) if k == 4 else every
                wait(G.at[here, :, got], g_r.at[d, p, k - 1])
            if k < 4:
                some = span(p, d) if k == 3 else every
                piece = G.at[here, :, some]
                send(piece, piece, g_s.at[d, p, k], g_r.at[d, p, k], ring[d])

    def gradient(p):
        cols = slice(p * voc // 2, (p + 1) * voc // 2)
        return lax.dot_general(
            G[:, :, cols].reshape(128, voc // 2), V[:, cols], (((1,), (1,)), ((), ())),
            preferred_element_type=F32,
        )

    for t in range(6):
        for k in (4, 3, 2, 1, 0):
            if 0 <= t - k < 2:
                grad_step(t - k, k)
        if t == 1:
            again = PRE[...].reshape(128, units).astype(F32)
            sig = 1.0 / (1.0 + jnp.exp(-again))
            D1[...] = sig * (1.0 + again * (1.0 - sig))
            ACC[...] = jnp.zeros_like(ACC)
        if t == 4:
            DR[...] = gradient(0)
    DQ[...] = ((DR[...] + gradient(1)) * D1[...]).astype(BF16).reshape(8, 16, units)

    slot = slot_of((x + 4 - shard // 4) % 4, (y_lo + (shard // 2) % 2) % 2)
    for g in range(8):
        device = in_source(g)
        place = DP.at[slot, 4 * flip + g // 2, g % 2 * 16:g % 2 * 16 + 16]

        @pl.when(is_self(device))
        def _(g=g, place=place):
            pltpu.make_async_copy(DQ.at[g], place, d_r.at[slot]).start()

        @pl.when(jnp.logical_not(is_self(device)))
        def _(g=g, place=place, device=device):
            send(DQ.at[g], place, d_s.at[g], d_r.at[slot], device)

    loss_out[...] = jnp.broadcast_to(
        jnp.sum(G[:, :, voc:].astype(F32), axis=2, keepdims=True), loss_out.shape
    )

    mt = min(256, units)

    def weight_tick(t, _):
        for k in (5, 4, 3, 2):
            rk = t - k

            @pl.when(live(rk, ROUNDS))
            def _(k=k, rk=rk):
                for d in (0, 1):
                    here = behind(d, k - 1)
                    half = slice(d * 16, d * 16 + 16)
                    if k == 5:
                        wait(DP.at[rk, here, half], a_r.at[d, rk, 3])
                        continue
                    wait(DP.at[rk, here], a_r.at[d, rk, k - 2])
                    piece = DP.at[rk, here, half] if k == 4 else DP.at[rk, here]
                    send(piece, piece, a_s.at[d, rk, k - 1], a_r.at[d, rk, k - 1], ring[d])

        r1 = t - 1

        @pl.when(live(r1, ROUNDS))
        def _():
            other = pl.ds(pl.multiple_of(16 - y_hi * 16, 16), 16)
            wait(DP.at[r1, z, other], dy_r.at[r1])
            piece = DP.at[r1, z]
            for d in (0, 1):
                send(piece, piece, a_s.at[d, r1, 0], a_r.at[d, r1, 0], ring[d])

        @pl.when(t < ROUNDS)
        def _():
            mine = pl.ds(pl.multiple_of(y_hi * 16, 16), 16)
            piece = DP.at[t, z, mine]
            wait(piece, d_r.at[t])
            send(piece, piece, dy_s.at[t], dy_r.at[t], y_far)

        r5 = t - 5

        @pl.when(live(r5, ROUNDS))
        def _():
            def tile(m, _):
                cols = pl.ds(pl.multiple_of(m * mt, mt), mt)
                ACC[cols, :] += lax.dot_general(
                    DP[r5, :, :, cols].reshape(256, mt), H[r5].reshape(256, feats),
                    (((0,), (0,)), ((), ())), preferred_element_type=F32,
                )
                return 0

            lax.fori_loop(0, units // mt, tile, 0)

        return 0

    lax.fori_loop(0, ROUNDS + 5, weight_tick, 0)

    def finish(m, _):
        rows = pl.ds(pl.multiple_of(m * mt, mt), mt)
        OUT[rows, :] = ACC[rows, :].astype(BF16)
        pltpu.make_async_copy(OUT.at[rows], out.at[rows], o_s.at[m]).start()
        return 0

    lax.fori_loop(0, units // mt, finish, 0)

    for n in range(7):
        wait(H.at[0, 0], h_far.at[n])

    def sent(r, _):
        wait(H.at[0, 0], h_sib.at[r])
        wait(YS.at[r], y_s.at[r])
        wait(DP.at[r, 0, 0:16], dy_s.at[r])

        @pl.when(jnp.logical_not(is_self(out_target(r))))
        def _():
            wait(TS.at[r], t_s.at[r])

        @pl.when(jnp.logical_not(is_self(in_source(r))))
        def _():
            wait(DQ.at[r], d_s.at[r])

        for d in (0, 1):
            wait(S0.at[d, r], rs_s.at[d, r, 0])
            wait(DP.at[r, 0, 0:16], a_s.at[d, r, 3])
            for k in range(3):
                wait(R.at[d, r, 0], rs_s.at[d, r, k + 1])
                wait(DP.at[r, 0], a_s.at[d, r, k])
        return 0

    lax.fori_loop(0, ROUNDS, sent, 0)

    def sent_logits(p, _):
        wait(LYS.at[p], ly_s.at[p])
        for d in (0, 1):
            wait(SL.at[d, p], l_s.at[d, p, 0])
            for k in range(3):
                wait(RL.at[d, p, 0], l_s.at[d, p, k + 1])
        return 0

    lax.fori_loop(0, PARTS, sent_logits, 0)
    for p in range(2):
        for d in (0, 1):
            for k in range(4):
                some = span(p, d) if k == 3 else slice(spans[p][0], spans[p][2])
                wait(G.at[0, :, some], g_s.at[d, p, k])
    for m in range(units // mt):
        rows = slice(m * mt, (m + 1) * mt)
        pltpu.make_async_copy(OUT.at[rows], out.at[rows], o_s.at[m]).wait()


def body(hidden, head_weight, vocab_head, targets):
    feats, units = head_weight.shape
    voc = vocab_head.shape[1]
    vq = voc // PARTS
    dma = pltpu.SemaphoreType.DMA
    vmem = pltpu.VMEM
    scratch = [
        vmem((ROUNDS, 2, 128, feats), BF16),
        vmem((feats, units), BF16),
        vmem((units, voc), BF16),
        vmem((ROUNDS, RING, 32, units), F32),
        vmem((2, ROUNDS, 16, units), BF16),
        vmem((2, ROUNDS, 4, 32, units), BF16),
        vmem((ROUNDS, 16, units), BF16),
        vmem((ROUNDS, 16, units), F32),
        vmem((ROUNDS, 16, units), BF16),
        vmem((ROUNDS, 16, units), BF16),
        vmem((8, 16, units), BF16),
        vmem((128, units), BF16),
        vmem((128, units), F32),
        vmem((PARTS, RING, 16, vq), F32),
        vmem((2, PARTS, 16, vq // 2), BF16),
        vmem((2, PARTS, 4, 16, vq), BF16),
        vmem((PARTS, 16, vq), BF16),
        vmem((PARTS, 16, vq), BF16),
        vmem((PARTS, 16, vq), F32),
        vmem((RING, 16, voc + 128), BF16),
        vmem((128, units), F32),
        vmem((8, 16, units), BF16),
        vmem((ROUNDS, RING, 32, units), BF16),
        vmem((units, feats), F32),
        vmem((units, feats), BF16),
        dma((3,)),
        dma((8,)), dma((7,)), dma((8, 2)),
        dma((2, ROUNDS, 4)), dma((2, ROUNDS, 4)),
        dma((ROUNDS,)), dma((ROUNDS,)),
        dma((ROUNDS,)), dma((8,)),
        dma((2, PARTS, 4)), dma((2, PARTS, 4)),
        dma((PARTS,)), dma((PARTS,)),
        dma((2, 2, 4)), dma((2, 2, 4)),
        dma((8,)), dma((ROUNDS,)),
        dma((ROUNDS,)), dma((ROUNDS,)),
        dma((2, ROUNDS, 4)), dma((2, ROUNDS, 4)),
        dma((max(1, units // 256),)),
    ]
    anywhere = pl.BlockSpec(memory_space=pl.ANY)
    inside = pl.BlockSpec(memory_space=pltpu.VMEM)
    grad, loss = pl.pallas_call(
        kernel,
        out_shape=[
            jax.ShapeDtypeStruct((units, feats), BF16),
            jax.ShapeDtypeStruct((RING, 16, 128), F32),
        ],
        in_specs=[anywhere, anywhere, anywhere, inside],
        out_specs=[anywhere, inside],
        scratch_shapes=scratch,
        compiler_params=pltpu.CompilerParams(
            collective_id=0, has_side_effects=True, vmem_limit_bytes=56 * 1024 * 1024
        ),
        name="head",
    )(hidden, head_weight, vocab_head, targets.reshape(RING, 16, 1))
    return grad, loss[:, :, 0].reshape(targets.shape)


def solution(mesh):
    in_specs = (P("dp", "shard"), P("shard", "dp"), P("shard", None), P("dp"))
    out_specs = (P("dp", "shard"), P("dp"))
    return jax.shard_map(body, mesh=mesh, in_specs=in_specs, out_specs=out_specs, check_vma=False)
```

time: 658 us -> 222 us (0.34)
  waiting for transfers between devices: 560 us -> 0 us
  Pallas kernels: 0 us -> 213 us
  blocking collectives: 32.6 us -> 0 us
  matrix products: 29.3 us -> 0 us
  between operations: 13.8 us -> 0.65 us
    pallas_call x0 -> x1, Pallas kernels: none -> 213 us  [body(): pl.pallas_call(kernel, out_shape=[jax.ShapeDtypeStruct((units, feats), BF...]
    reduce_scatter x1 -> x0, waiting for transfers between devices: 211 us -> none  [body(): lax.psum_scatter(jnp.transpose(term, (1, 0, 2, 3)).reshape(per_group * la...]
    psum x1 -> x0, waiting for transfers between devices: 154 us -> none  [body(): lax.psum(partial_logits.astype(jnp.bfloat16), 'shard').astype(jnp.float32)]
    all_gather x2 -> x0, waiting for transfers between devices: 143 us -> none  [the longest x1 98.3 us: body(): full_units = lax.all_gather(dpre, 'shard', axis=1, tiled=True)]
    all_to_all x1 -> x0, waiting for transfers between devices: 51.5 us -> none  [body(): lax.all_to_all(full_units, 'dp', split_axis=1, concat_axis=0, tiled=True)]
    all_to_all x2 -> x0, blocking collectives: 32.6 us -> none  [the longest x1 20.6 us: body(): lax.all_to_all(lax.all_to_all(middle.astype(jnp.bfloat16), 'dp', split_ax...]
    dot_general x4 -> x0, matrix products: 29.3 us -> none  [the longest x1 9.36 us: body(): lax.dot_general(columns, all_hidden, (((0,), (0,)), ((), ())), preferred_...]
  transfers between devices with their start and end apart: 5 -> 0, of which waited for: 5 -> 0; matrix products, arithmetic and copies ran while one was open for 0% -> 0% of each run, Pallas kernels for 0% -> 0%
where the time goes in v1:
time: 222 us; the launch traced here: 220 us
  Pallas kernels  213 us (96%)
  local copies, waits for them, and re-layouts  6.09 us (3%)
    pallas_call x1, Pallas kernels, body(): pl.pallas_call(kernel, out_shape=[jax.ShapeDtypeStruct((units, feats), BF...  213 us

profile of v1, /device:TPU:32, one launch (start us, length us, event | category | flops | bytes accessed | tf_op | source)
XLA Modules:
  0.0 219.5 jit_solution(5840060519484001674)
XLA Ops:
  0.6 1.5 reshape.8.tgt
  2.1 212.8 %head.1 = (bf16[1024,1024]{1,0:T(8,128)(2,1)}, f32[8,16,128]{2,1,0:T(8,128)}) custom-call(bf16[128,1024]{1,0:T(8,128)(2,1)} %h_in.1, bf16[1024,1024]{1,0:T(8,128)(2,1)} %w_in.1, bf16[1024,4096]{1,0:T(8,128)(2,1)} %v_in.1, s32[8,16,1]{2,1,0:T(8,128)} %reshape.8.tgt), custom_call_target="tpu_custom_call" | custom-call | tf_op jit(solution)/shard_map/head/pallas_call | solution.py:511
  214.9 0.9 slice_reduce_fusion
  215.8 0.6 reshape_squeeze.3
  216.4 3.1 %copy.9 = bf16[1024,1024]{1,0:T(8,128)(2,1)} copy(bf16[1024,1024]{1,0:T(8,128)(2,1)} %get-tuple-element.8) | data formatting | bytes 4194304

commit v2 on v0

v2 whole, which is shorter than its diff:
```python
import jax
import jax.numpy as jnp
from jax import lax
from jax.experimental import pallas as pl
from jax.experimental.pallas import tpu as pltpu
from jax.sharding import PartitionSpec as P

MESH = pl.DeviceIdType.MESH
BF16 = jnp.bfloat16
F32 = jnp.float32

ROUNDS = 8
RING = 8
PARTS = 4


def slot_of(dx, a):
    odd = dx % 2
    return odd * (2 + 2 * a + (3 - dx) // 2) + (1 - odd) * (3 * dx + a)


def offset_of(slot):
    middle = jnp.logical_and(slot >= 2, slot <= 5)
    dx = jnp.where(middle, 3 - 2 * (slot % 2), jnp.where(slot >= 6, 2, 0))
    a = jnp.where(middle, (slot // 2 + 1) % 2, slot % 2)
    return dx, a


def send(src, dst, send_sem, recv_sem, device):
    pltpu.make_async_remote_copy(
        src_ref=src,
        dst_ref=dst,
        send_sem=send_sem,
        recv_sem=recv_sem,
        device_id=device,
        device_id_type=MESH,
    ).start()


def wait(ref, sem):
    pltpu.make_async_copy(ref, ref, sem).wait()


def kernel(
    h_in, w_in, v_in, tgt, out, loss_out,
    H, W, V, PT, S0, R, YS, YK, YR, YB, YC, TS, PRE, RES, D1, L, SL, RL, LYS, LYR, LF, G, LT, DR, DQ, DP,
    ACC, OUT,
    loc, h_s, h_r, rs_s, rs_r, y_s, y_r, yc_r, t_s, t_r, l_s, l_r, ly_s, ly_r, g_s, g_r, lt_s, lt_r,
    d_s, d_r, dy_s, dy_r, a_s, a_r, o_s,
):
    dp = lax.axis_index("dp")
    shard = lax.axis_index("shard")
    x, y_lo, core = dp // 4, (dp // 2) % 2, dp % 2
    z, y_hi = shard // 2, shard % 2
    y_other = 1 - y_hi
    feats = H.shape[2]
    units = W.shape[1]
    vq = L.shape[3]
    hu, hc = units // 2, vq // 2

    x_next = ((dp + 4) % 16, shard)
    x_prev = ((dp + 12) % 16, shard)
    y_near = (dp + 2 - 4 * y_lo, shard)
    sibling = (dp + 1 - 2 * core, shard)
    z_next = (dp, (shard + 2) % 16)
    z_prev = (dp, (shard + 14) % 16)
    y_far = (dp, shard + 1 - 2 * y_hi)
    ring = (z_next, z_prev)

    def out_target(slot):
        dx, a = offset_of(slot)
        there = ((x + dx) % 4) * 4 + ((y_lo + a) % 2) * 2 + (core + y_hi) % 2
        return (there, dp)

    flip = (core + shard % 2) % 2

    def in_source(g):
        return (shard, 2 * g + flip)

    def is_self(device):
        return jnp.logical_and(device[0] == dp, device[1] == shard)

    own = jnp.logical_and(dp == shard, y_hi == 0)

    barrier = pltpu.get_barrier_semaphore()
    near = (x_next, x_prev, y_near, sibling, z_next, z_prev, y_far)
    for device in near:
        pl.semaphore_signal(barrier, inc=1, device_id=device, device_id_type=MESH)
    copy_w = pltpu.make_async_copy(w_in, W, loc.at[0])
    copy_w.start()
    copy_h = pltpu.make_async_copy(h_in, H.at[0], loc.at[2])
    copy_h.start()
    copy_v = pltpu.make_async_copy(v_in, V, loc.at[1])
    pl.semaphore_wait(barrier, len(near))

    def pass_on(src, slot, device):
        send(src, H.at[slot], h_s, h_r.at[slot], device)

    pass_on(h_in, 1, sibling)
    pass_on(h_in, 2, y_near)
    pass_on(h_in, 4, x_next)
    pass_on(h_in, 6, x_prev)
    copy_v.start()

    def service(q):
        wait(H.at[2 * q], h_r.at[2 * q])
        pass_on(H.at[2 * q], 2 * q + 1, sibling)

        @pl.when(q == 1)
        def _():
            pass_on(H.at[2], 8, x_next)
            pass_on(H.at[2], 10, x_prev)

        @pl.when(q == 2)
        def _():
            pass_on(H.at[4], 12, x_next)

        @pl.when(q == 5)
        def _():
            pass_on(H.at[10], 14, x_prev)

    copy_h.wait()
    copy_w.wait()

    def ahead(d, k):
        return (z + (RING // 2 - k if d == 0 else RING // 2 + k)) % RING

    def behind(d, k):
        return (z + (RING - k if d == 0 else k)) % RING

    def live(r, n):
        return jnp.logical_and(r >= 0, r < n)

    nt = min(512, units)

    def product(t):
        def tile(n, _):
            cols = pl.ds(pl.multiple_of(n * nt, nt), nt)
            rows = H[pl.ds(2 * t, 2)].reshape(256, feats)
            PT[t, :, :, :, cols] = jnp.dot(
                rows, W[:, cols], preferred_element_type=F32
            ).reshape(2, RING, 16, nt)
            return 0

        lax.fori_loop(0, units // nt, tile, 0)

    def even_step(r, s):
        q = r // 2
        if s == 0:
            for d in (0, 1):
                S0[d, r] = PT[r, d, ahead(d, 0)].astype(BF16)
                send(S0.at[d, r], R.at[d, r, 0, d], rs_s.at[0], rs_r.at[d, r, 0], ring[d])
        elif s < 4:
            for d in (0, 1):
                at = ahead(d, s)
                if s == 1:
                    wait(R.at[d, r, 0, d], rs_r.at[d, r, 0])
                    R[d, r, 0, d] = (PT[r, d, at] + R[d, r, 0, d].astype(F32)).astype(BF16)
                    R[d, r, 0, 1 - d] = PT[r, 1 - d, at].astype(BF16)
                else:
                    wait(R.at[d, r, s - 1], rs_r.at[d, r, s - 1])
                    R[d, r, s - 1] = (PT[r, :, at] + R[d, r, s - 1].astype(F32)).astype(BF16)
                send(R.at[d, r, s - 1], R.at[d, r, s], rs_s.at[1], rs_r.at[d, r, s], ring[d])
        elif s == 4:
            wait(R.at[0, r, 3], rs_r.at[0, r, 3])
            wait(R.at[1, r, 3], rs_r.at[1, r, 3])

            def total(h):
                return PT[r, h, z] + R[0, r, 3, h].astype(F32) + R[1, r, 3, h].astype(F32)

            YS[q] = total(y_other).astype(BF16)
            send(YS.at[q], YR.at[q], y_s.at[0], y_r.at[q], y_far)
            YK[q] = total(y_hi)
        else:
            wait(YR.at[q], y_r.at[q])
            TS[r] = (YK[q] + YR[q].astype(F32)).astype(BF16)

    groups = ((0, 1), (1, 3), (3, 5), (5, 7), (7, 8))

    def odd_step(r, s):
        q = r // 2
        if s == 0:
            for n, (low, high) in enumerate(groups):
                YB[q, low] = PT[r, y_other, ahead(0, n)].astype(BF16)
                if high - low == 2:
                    YB[q, low + 1] = PT[r, y_other, ahead(1, n)].astype(BF16)
                send(YB.at[q, low:high], YC.at[q, low:high], y_s.at[1], yc_r.at[q, n], y_far)
            return
        k = s - 1
        low, high = groups[k]
        wait(YC.at[q, low:high], yc_r.at[q, k])

        def mine(d, cols=slice(None)):
            return PT[r, y_hi, ahead(d, k), :, cols] + YC[q, low if high - low == 1 else low + d, :, cols].astype(F32)

        if k == 4:
            wait(R.at[0, r, 3, 0], rs_r.at[0, r, 3])
            wait(R.at[1, r, 3, 0], rs_r.at[1, r, 3])
            TS[r] = (mine(0) + R[0, r, 3, 0].astype(F32) + R[1, r, 3, 0].astype(F32)).astype(BF16)
            return
        for d in (0, 1):
            half = slice(d * hu, d * hu + hu)
            rest = slice(hu - d * hu, 2 * hu - d * hu)
            if k == 0:
                S0[d, r, :, half] = mine(d, half).astype(BF16)
                send(S0.at[d, r, :, half], R.at[d, r, 0, 0, :, half], rs_s.at[2], rs_r.at[d, r, 0], ring[d])
                continue
            if k == 1:
                wait(R.at[d, r, 0, 0, :, half], rs_r.at[d, r, 0])
                R[d, r, 0, 0, :, half] = (mine(d, half) + R[d, r, 0, 0, :, half].astype(F32)).astype(BF16)
                R[d, r, 0, 0, :, rest] = mine(d, rest).astype(BF16)
            else:
                wait(R.at[d, r, k - 1, 0], rs_r.at[d, r, k - 1])
                R[d, r, k - 1, 0] = (mine(d) + R[d, r, k - 1, 0].astype(F32)).astype(BF16)
            send(R.at[d, r, k - 1, 0], R.at[d, r, k, 0], rs_s.at[3], rs_r.at[d, r, k], ring[d])

    def hand_over(r):
        device = out_target(r)

        @pl.when(is_self(device))
        def _():
            pltpu.make_async_copy(TS.at[r], PRE.at[z], t_r).start()

        @pl.when(jnp.logical_not(is_self(device)))
        def _():
            send(TS.at[r], PRE.at[z], t_s, t_r, device)

    def pre_ticks(pair, _):
        for u in (0, 1):
            t = 2 * pair + u
            for s in (5, 4, 3, 2, 1):
                @pl.when(live(t - s, ROUNDS))
                def _(s=s, t=t, u=u):
                    (odd_step if (u - s) % 2 else even_step)(t - s, s)

            if u == 1:
                @pl.when(t == 1)
                def _(t=t):
                    service(t)

            @pl.when(t < ROUNDS)
            def _(t=t, u=u):
                wait(H.at[2 * t + 1], h_r.at[2 * t + 1])
                product(t)
                (odd_step if u else even_step)(t, 0)

            @pl.when(jnp.logical_and(t >= 1, t < ROUNDS - 1))
            def _(t=t):
                service(t + 1)

            @pl.when(t == 1)
            def _():
                ACC[...] = jnp.zeros_like(ACC)

            @pl.when(jnp.logical_and(t >= 8, t <= 10))
            def _(t=t):
                hand_over(2 * (t - 8))
                hand_over(2 * (t - 8) + 1)

            @pl.when(jnp.logical_and(t >= 11, t <= 12))
            def _(t=t):
                hand_over(t - 5)

        return 0

    lax.fori_loop(0, ROUNDS // 2 + 3, pre_ticks, 0)

    wait(PRE, t_r)
    pre = PRE[...].reshape(128, units).astype(F32)
    RES[...] = (H[0].astype(F32) + pre / (1.0 + jnp.exp(-pre))).astype(BF16)
    copy_v.wait()

    def logit_step(p, k):
        if k == 5:
            wait(LYR.at[p], ly_r.at[p])
            LF[p] = LYS[p].astype(F32) + LYR[p].astype(F32)
            return
        if k == 4:
            wait(RL.at[0, p, 3], l_r.at[0, p, 3])
            wait(RL.at[1, p, 3], l_r.at[1, p, 3])
            LYS[p] = (L[p, z] + RL[0, p, 3].astype(F32) + RL[1, p, 3].astype(F32)).astype(BF16)
            send(LYS.at[p], LYR.at[p], ly_s, ly_r.at[p], y_far)
            return
        for d in (0, 1):
            at = ahead(d, k)
            half = slice(d * hc, d * hc + hc)
            rest = slice(hc - d * hc, 2 * hc - d * hc)
            if k == 0:
                SL[d, p] = L[p, at, :, half].astype(BF16)
                send(SL.at[d, p], RL.at[d, p, 0, :, half], l_s.at[0], l_r.at[d, p, 0], ring[d])
                continue
            if k == 1:
                wait(RL.at[d, p, 0, :, half], l_r.at[d, p, 0])
                RL[d, p, 0, :, half] = (L[p, at, :, half] + RL[d, p, 0, :, half].astype(F32)).astype(BF16)
                RL[d, p, 0, :, rest] = L[p, at, :, rest].astype(BF16)
            else:
                wait(RL.at[d, p, k - 1], l_r.at[d, p, k - 1])
                RL[d, p, k - 1] = (L[p, at] + RL[d, p, k - 1].astype(F32)).astype(BF16)
            send(RL.at[d, p, k - 1], RL.at[d, p, k], l_s.at[1], l_r.at[d, p, k], ring[d])

    def logit_tick(t, _):
        @pl.when(t < PARTS)
        def _():
            cols = pl.ds(pl.multiple_of(t * vq, vq), vq)
            L[t] = jnp.dot(RES[...], V[:, cols], preferred_element_type=F32).reshape(RING, 16, vq)
            logit_step(t, 0)

        for k in (5, 4, 3, 2, 1):
            @pl.when(live(t - k, PARTS))
            def _(k=k):
                logit_step(t - k, k)

        @pl.when(t == 4)
        def _():
            again = PRE[...].reshape(128, units).astype(F32)
            sig = 1.0 / (1.0 + jnp.exp(-again))
            D1[...] = sig * (1.0 + again * (1.0 - sig))

        return 0

    lax.fori_loop(0, PARTS + 5, logit_tick, 0)

    total = jnp.zeros((16, 1), F32)
    picked = jnp.zeros((16, 1), F32)
    spot = lax.broadcasted_iota(jnp.int32, (16, 128), 0) + z * 16
    lane = lax.broadcasted_iota(jnp.int32, (16, 128), 1)
    target = jnp.sum(jnp.where(spot == lane, tgt[...], 0), axis=1, keepdims=True)
    for p in range(PARTS):
        logits = LF[p]
        hit = lax.broadcasted_iota(jnp.int32, (16, vq), 1) + p * vq == target
        total += jnp.sum(jnp.exp(logits), axis=1, keepdims=True)
        picked += jnp.sum(jnp.where(hit, logits, 0.0), axis=1, keepdims=True)

    def grad_step(p, k):
        for d in (0, 1):
            here = behind(d, k)
            half = slice(d * hc, d * hc + hc)
            if k > 0:
                piece = G.at[p, here, :, half] if k == 4 else G.at[p, here]
                wait(piece, g_r.at[d, p, k - 1])
            if k < 4:
                piece = G.at[p, here, :, half] if k == 3 else G.at[p, here]
                send(piece, piece, g_s.at[k // 3], g_r.at[d, p, k], ring[d])

    def loss_step(k):
        for d in (0, 1):
            here = behind(d, k)
            if k > 0 and (d == 0 or k < 4):
                wait(LT.at[here], lt_r.at[d, k - 1])
            if k < 3 or (k == 3 and d == 0):
                send(LT.at[here], LT.at[here], lt_s, lt_r.at[d, k], ring[d])

    for p in range(PARTS):
        hit = lax.broadcasted_iota(jnp.int32, (16, vq), 1) + p * vq == target
        G[p, z] = (jnp.exp(LF[p]) / total - jnp.where(hit, 1.0, 0.0)).astype(BF16)
        grad_step(p, 0)
    loss = jnp.log(total) - picked
    high = loss.astype(BF16).astype(F32)
    middle = (loss - high).astype(BF16).astype(F32)
    low = loss - high - middle
    LT[z] = jnp.where(
        lane == 0, high, jnp.where(lane == 1, middle, jnp.where(lane == 2, low, 0.0))
    ).astype(BF16)
    loss_step(0)

    def gradient_tick(t, _):
        for k in (3, 2, 1):
            @pl.when(live(t - k, PARTS))
            def _(k=k):
                grad_step(t - k, k)

        @pl.when(live(t - 4, PARTS))
        def _():
            p = t - 4
            grad_step(p, 4)
            cols = pl.ds(pl.multiple_of(p * vq, vq), vq)
            part = lax.dot_general(
                G[p].reshape(128, vq), V[:, cols], (((1,), (1,)), ((), ())),
                preferred_element_type=F32,
            )
            DR[...] = jnp.where(p == 0, part, DR[...] + part)

        return 0

    DR[...] = jnp.zeros_like(DR)
    lax.fori_loop(1, PARTS + 4, gradient_tick, 0)
    DQ[...] = (DR[...] * D1[...]).astype(BF16).reshape(8, 16, units)

    slot = slot_of((x + 4 - shard // 4) % 4, (y_lo + (shard // 2) % 2) % 2)
    for g in range(8):
        device = in_source(g)
        place = DP.at[slot, flip, g]

        @pl.when(is_self(device))
        def _(g=g, place=place):
            pltpu.make_async_copy(DQ.at[g], place, d_r.at[slot]).start()

        @pl.when(jnp.logical_not(is_self(device)))
        def _(g=g, place=place, device=device):
            send(DQ.at[g], place, d_s, d_r.at[slot], device)

    for k in range(1, 5):
        loss_step(k)
    column = jnp.sum(LT[...].reshape(128, 128).astype(F32), axis=1, keepdims=True)
    diagonal = lax.broadcasted_iota(jnp.int32, (128, 128), 0) == lax.broadcasted_iota(jnp.int32, (128, 128), 1)
    loss_out[...] = jnp.sum(jnp.where(diagonal, column, 0.0), axis=0, keepdims=True)

    mt = min(256, units)

    def over_y(piece, r, n):
        send(piece, piece, dy_s.at[n], dy_r.at[r], y_far)

    def even_gather(r, s):
        if s == 5:
            wait(DP.at[r, y_other], dy_r.at[r])
            return
        if s == 0:
            piece = DP.at[r, y_hi, z]
            wait(piece, d_r.at[r])
            for d in (0, 1):
                send(piece, piece, a_s.at[0], a_r.at[d, r, 0], ring[d])
            over_y(piece, r, 0)
            return
        for d in (0, 1):
            here = behind(d, s)
            piece = DP.at[r, y_hi, here]
            half = DP.at[r, y_hi, here, :, d * hu:d * hu + hu]
            if s == 4:
                wait(half, a_r.at[d, r, 3])
                continue
            wait(piece, a_r.at[d, r, s - 1])
            if s == 3:
                send(half, half, a_s.at[1], a_r.at[d, r, 3], ring[d])
            else:
                send(piece, piece, a_s.at[0], a_r.at[d, r, s], ring[d])
            over_y(piece, r, 0)
        if s == 4:
            over_y(DP.at[r, y_hi, behind(0, 4)], r, 0)

    def odd_gather(r, s):
        if s == 0:
            piece = DP.at[r, y_hi, z]
            wait(piece, d_r.at[r])
            over_y(piece, r, 1)
            return
        if s == 1:
            wait(DP.at[r, y_other, z], dy_r.at[r])
        for d in (0, 1):
            here = behind(d, s - 1)
            piece = DP.at[r, :, here]
            half = DP.at[r, d, here]
            if s == 5:
                wait(half, a_r.at[d, r, 3])
                continue
            if s > 1:
                wait(piece, a_r.at[d, r, s - 2])
            if s == 4:
                send(half, half, a_s.at[3], a_r.at[d, r, 3], ring[d])
            else:
                send(piece, piece, a_s.at[2], a_r.at[d, r, s - 1], ring[d])

    def outer(r, m):
        cols = pl.ds(pl.multiple_of(m * mt, mt), mt)
        return lax.dot_general(
            DP[r, :, :, :, cols].reshape(256, mt), H[pl.ds(2 * r, 2)].reshape(256, feats),
            (((0,), (0,)), ((), ())), preferred_element_type=F32,
        )

    def weight_ticks(pair, _):
        for u in (0, 1):
            t = 2 * pair + u
            for s in (4, 3, 2, 1, 0, 5):
                @pl.when(live(t - s, ROUNDS))
                def _(s=s, t=t, u=u):
                    (odd_gather if (u - s) % 2 else even_gather)(t - s, s)

            @pl.when(live(t - 5, ROUNDS - 1))
            def _(t=t):
                def tile(m, _):
                    rows = pl.ds(pl.multiple_of(m * mt, mt), mt)
                    ACC[rows, :] += outer(t - 5, m)
                    return 0

                lax.fori_loop(0, units // mt, tile, 0)

        return 0

    lax.fori_loop(0, ROUNDS // 2 + 3, weight_ticks, 0)

    def finish(m, _):
        rows = pl.ds(pl.multiple_of(m * mt, mt), mt)
        OUT[rows, :] = (ACC[rows, :] + outer(ROUNDS - 1, m)).astype(BF16)
        pltpu.make_async_copy(OUT.at[rows], out.at[rows], o_s).start()
        return 0

    lax.fori_loop(0, units // mt, finish, 0)

    four = DP.at[0, 0, 0:4]
    eight = DP.at[0, 0]
    wait(H.at[0:15], h_s)
    wait(eight, rs_s.at[0])
    wait(DP.at[0:3], rs_s.at[1])
    wait(four, rs_s.at[2])
    wait(DP.at[0:3, 0], rs_s.at[3])
    wait(four, y_s.at[0])
    wait(DP.at[0:2], y_s.at[1])
    wait(DP.at[0:3, 0], a_s.at[0])
    wait(four, a_s.at[1])
    wait(DP.at[0:3], a_s.at[2])
    wait(eight, a_s.at[3])
    wait(DP.at[0:2], dy_s.at[0])
    wait(four, dy_s.at[1])
    wait(SL, l_s.at[0])
    wait(RL.at[:, 0:3], l_s.at[1])
    wait(LYS, ly_s)
    wait(G.at[0:3], g_s.at[0])
    wait(G.at[0, 0:4], g_s.at[1])
    wait(LT.at[0:7], lt_s)

    @pl.when(own)
    def _():
        wait(DP.at[0, 0, 0:7], t_s)
        wait(DP.at[0, 0, 0:7], d_s)

    @pl.when(jnp.logical_not(own))
    def _():
        wait(eight, t_s)
        wait(eight, d_s)

    pltpu.make_async_copy(OUT, out, o_s).wait()


def body(hidden, head_weight, vocab_head, targets):
    feats, units = head_weight.shape
    voc = vocab_head.shape[1]
    vq = voc // PARTS
    pairs = ROUNDS // 2
    dma = pltpu.SemaphoreType.DMA
    one = pltpu.SemaphoreType.DMA
    vmem = pltpu.VMEM
    scratch = [
        vmem((2 * ROUNDS, 128, feats), BF16),
        vmem((feats, units), BF16),
        vmem((units, voc), BF16),
        vmem((ROUNDS, 2, RING, 16, units), F32),
        vmem((2, ROUNDS, 16, units), BF16),
        vmem((2, ROUNDS, 4, 2, 16, units), BF16),
        vmem((pairs, 16, units), BF16),
        vmem((pairs, 16, units), F32),
        vmem((pairs, 16, units), BF16),
        vmem((pairs, RING, 16, units), BF16),
        vmem((pairs, RING, 16, units), BF16),
        vmem((ROUNDS, 16, units), BF16),
        vmem((8, 16, units), BF16),
        vmem((128, units), BF16),
        vmem((128, units), F32),
        vmem((PARTS, RING, 16, vq), F32),
        vmem((2, PARTS, 16, vq // 2), BF16),
        vmem((2, PARTS, 4, 16, vq), BF16),
        vmem((PARTS, 16, vq), BF16),
        vmem((PARTS, 16, vq), BF16),
        vmem((PARTS, 16, vq), F32),
        vmem((PARTS, RING, 16, vq), BF16),
        vmem((RING, 16, 128), BF16),
        vmem((128, units), F32),
        vmem((8, 16, units), BF16),
        vmem((ROUNDS, 2, RING, 16, units), BF16),
        vmem((units, feats), F32),
        vmem((units, feats), BF16),
        dma((3,)),
        one, dma((2 * ROUNDS,)),
        dma((4,)), dma((2, ROUNDS, 4)),
        dma((2,)), dma((pairs,)), dma((pairs, 5)),
        one, one,
        dma((2,)), dma((2, PARTS, 4)),
        one, dma((PARTS,)),
        dma((2,)), dma((2, PARTS, 4)),
        one, dma((2, 4)),
        one, dma((ROUNDS,)),
        dma((2,)), dma((ROUNDS,)),
        dma((4,)), dma((2, ROUNDS, 4)),
        one,
    ]
    anywhere = pl.BlockSpec(memory_space=pl.ANY)
    inside = pl.BlockSpec(memory_space=pltpu.VMEM)
    grad, loss = pl.pallas_call(
        kernel,
        out_shape=[
            jax.ShapeDtypeStruct((units, feats), BF16),
            jax.ShapeDtypeStruct((1, 128), F32),
        ],
        in_specs=[anywhere, anywhere, anywhere, inside],
        out_specs=[anywhere, inside],
        scratch_shapes=scratch,
        compiler_params=pltpu.CompilerParams(
            collective_id=0, has_side_effects=True, vmem_limit_bytes=58 * 1024 * 1024
        ),
        name="head",
    )(hidden, head_weight, vocab_head, targets.reshape(1, 128))
    return grad, loss.reshape(targets.shape)


def solution(mesh):
    in_specs = (P("dp", "shard"), P("shard", "dp"), P("shard", None), P("dp"))
    out_specs = (P("dp", "shard"), P("dp"))
    return jax.shard_map(body, mesh=mesh, in_specs=in_specs, out_specs=out_specs, check_vma=False)
```

time: 658 us -> 215 us (0.33); the launches traced: 651 us -> 214 us
  waiting for transfers between devices: 560 us -> 0 us
  Pallas kernels: 0 us -> 210 us
  blocking collectives: 32.6 us -> 0 us
  matrix products: 29.3 us -> 0 us
  between operations: 13.8 us -> 0.65 us
    reduce_scatter x1 -> x0, waiting for transfers between devices: 211 us -> none  [body(): lax.psum_scatter(jnp.transpose(term, (1, 0, 2, 3)).reshape(per_group * la...]
    pallas_call x0 -> x1, Pallas kernels: none -> 210 us  [body(): pl.pallas_call(kernel, out_shape=[jax.ShapeDtypeStruct((units, feats), BF...]
    psum x1 -> x0, waiting for transfers between devices: 154 us -> none  [body(): lax.psum(partial_logits.astype(jnp.bfloat16), 'shard').astype(jnp.float32)]
    all_gather x2 -> x0, waiting for transfers between devices: 143 us -> none  [the longest x1 98.3 us: body(): full_units = lax.all_gather(dpre, 'shard', axis=1, tiled=True)]
    all_to_all x1 -> x0, waiting for transfers between devices: 51.5 us -> none  [body(): lax.all_to_all(full_units, 'dp', split_axis=1, concat_axis=0, tiled=True)]
    all_to_all x2 -> x0, blocking collectives: 32.6 us -> none  [the longest x1 20.6 us: body(): lax.all_to_all(lax.all_to_all(middle.astype(jnp.bfloat16), 'dp', split_ax...]
    dot_general x4 -> x0, matrix products: 29.3 us -> none  [the longest x1 9.36 us: body(): lax.dot_general(columns, all_hidden, (((0,), (0,)), ((), ())), preferred_...]
  transfers between devices with their start and end apart: 5 -> 0, of which waited for: 5 -> 0; matrix products, arithmetic and copies ran while one was open for 0% -> 0% of each run, Pallas kernels for 0% -> 0%
where the time goes in v2:
time: 215 us; the launch traced here: 214 us
  Pallas kernels  210 us (98%)
  local copies, waits for them, and re-layouts  3.6 us (2%)
    pallas_call x1, Pallas kernels, body(): pl.pallas_call(kernel, out_shape=[jax.ShapeDtypeStruct((units, feats), BF...  210 us

profile of v2, /device:TPU:32, one launch (start us, length us, event | category | flops | bytes accessed | tf_op | source)
XLA Modules:
  0.0 214.4 jit_solution(2255502826945956487)
XLA Ops:
  0.6 210.2 %head.1 = (bf16[1024,1024]{1,0:T(8,128)(2,1)}, f32[1,128]{1,0:T(1,128)}) custom-call(bf16[128,1024]{1,0:T(8,128)(2,1)} %h_in.1, bf16[1024,1024]{1,0:T(8,128)(2,1)} %w_in.1, bf16[1024,4096]{1,0:T(8,128)(2,1)} %v_in.1, s32[1,128]{1,0:T(1,128)} %bitcast.2), custom_call_target="tpu_custom_call" | custom-call | tf_op jit(solution)/shard_map/head/pallas_call | solution.py:586
  210.8 0.0 copy-start
  210.8 3.1 %copy.8 = bf16[1024,1024]{1,0:T(8,128)(2,1)} copy(bf16[1024,1024]{1,0:T(8,128)(2,1)} %get-tuple-element.8) | data formatting | bytes 4194304
  213.9 0.0 copy-done
  213.9 0.5 copy.9
Async XLA Ops:
  210.8 3.1 %copy-start = (f32[1,128]{1,0:T(1,128)S(1)}, f32[1,128]{1,0:T(1,128)}, u32[]{:S(2)}) copy-start(f32[1,128]{1,0:T(1,128)} %get-tuple-element.5) | copy-start | bytes 1540

commit v3 on v2

--- a/solution.py
+++ b/solution.py
@@ -12,6 +12,7 @@
 ROUNDS = 8
 RING = 8
 PARTS = 4
+PRE_LAG, LOGIT_LAG, GRAD_LAG, WEIGHT_LAG = 2, 4, 4, 3
 
 
 def slot_of(dx, a):
@@ -229,9 +230,9 @@
         for u in (0, 1):
             t = 2 * pair + u
             for s in (5, 4, 3, 2, 1):
-                @pl.when(live(t - s, ROUNDS))
+                @pl.when(live(t - PRE_LAG * s, ROUNDS))
                 def _(s=s, t=t, u=u):
-                    (odd_step if (u - s) % 2 else even_step)(t - s, s)
+                    (odd_step if (u - PRE_LAG * s) % 2 else even_step)(t - PRE_LAG * s, s)
 
             if u == 1:
                 @pl.when(t == 1)
@@ -252,18 +253,20 @@
             def _():
                 ACC[...] = jnp.zeros_like(ACC)
 
-            @pl.when(jnp.logical_and(t >= 8, t <= 10))
-            def _(t=t):
-                hand_over(2 * (t - 8))
-                hand_over(2 * (t - 8) + 1)
-
-            @pl.when(jnp.logical_and(t >= 11, t <= 12))
-            def _(t=t):
-                hand_over(t - 5)
+            e = t - 5 * (PRE_LAG - 1)
+
+            @pl.when(jnp.logical_and(e >= 8, e <= 10))
+            def _(e=e):
+                hand_over(2 * (e - 8))
+                hand_over(2 * (e - 8) + 1)
+
+            @pl.when(jnp.logical_and(e >= 11, e <= 12))
+            def _(e=e):
+                hand_over(e - 5)
 
         return 0
 
-    lax.fori_loop(0, ROUNDS // 2 + 3, pre_ticks, 0)
+    lax.fori_loop(0, (ROUNDS + 5 * PRE_LAG + 1) // 2, pre_ticks, 0)
 
     wait(PRE, t_r)
     pre = PRE[...].reshape(128, units).astype(F32)
@@ -306,9 +309,9 @@
             logit_step(t, 0)
 
         for k in (5, 4, 3, 2, 1):
-            @pl.when(live(t - k, PARTS))
+            @pl.when(live(t - LOGIT_LAG * k, PARTS))
             def _(k=k):
-                logit_step(t - k, k)
+                logit_step(t - LOGIT_LAG * k, k)
 
         @pl.when(t == 4)
         def _():
@@ -318,7 +321,7 @@
 
         return 0
 
-    lax.fori_loop(0, PARTS + 5, logit_tick, 0)
+    lax.fori_loop(0, PARTS + 5 * LOGIT_LAG, logit_tick, 0)
 
     total = jnp.zeros((16, 1), F32)
     picked = jnp.zeros((16, 1), F32)
@@ -365,13 +368,13 @@
 
     def gradient_tick(t, _):
         for k in (3, 2, 1):
-            @pl.when(live(t - k, PARTS))
+            @pl.when(live(t - GRAD_LAG * k, PARTS))
             def _(k=k):
-                grad_step(t - k, k)
-
-        @pl.when(live(t - 4, PARTS))
-        def _():
-            p = t - 4
+                grad_step(t - GRAD_LAG * k, k)
+
+        @pl.when(live(t - 4 * GRAD_LAG, PARTS))
+        def _():
+            p = t - 4 * GRAD_LAG
             grad_step(p, 4)
             cols = pl.ds(pl.multiple_of(p * vq, vq), vq)
             part = lax.dot_general(
@@ -383,7 +386,7 @@
         return 0
 
     DR[...] = jnp.zeros_like(DR)
-    lax.fori_loop(1, PARTS + 4, gradient_tick, 0)
+    lax.fori_loop(1, PARTS + 4 * GRAD_LAG, gradient_tick, 0)
     DQ[...] = (DR[...] * D1[...]).astype(BF16).reshape(8, 16, units)
 
     slot = slot_of((x + 4 - shard // 4) % 4, (y_lo + (shard // 2) % 2) % 2)
@@ -470,22 +473,22 @@
         for u in (0, 1):
             t = 2 * pair + u
             for s in (4, 3, 2, 1, 0, 5):
-                @pl.when(live(t - s, ROUNDS))
+                @pl.when(live(t - WEIGHT_LAG * s, ROUNDS))
                 def _(s=s, t=t, u=u):
-                    (odd_gather if (u - s) % 2 else even_gather)(t - s, s)
-
-            @pl.when(live(t - 5, ROUNDS - 1))
+                    (odd_gather if (u - WEIGHT_LAG * s) % 2 else even_gather)(t - WEIGHT_LAG * s, s)
+
+            @pl.when(live(t - 5 * WEIGHT_LAG, ROUNDS - 1))
             def _(t=t):
                 def tile(m, _):
                     rows = pl.ds(pl.multiple_of(m * mt, mt), mt)
-                    ACC[rows, :] += outer(t - 5, m)
+                    ACC[rows, :] += outer(t - 5 * WEIGHT_LAG, m)
                     return 0
 
                 lax.fori_loop(0, units // mt, tile, 0)
 
         return 0
 
-    lax.fori_loop(0, ROUNDS // 2 + 3, weight_ticks, 0)
+    lax.fori_loop(0, (ROUNDS + 5 * WEIGHT_LAG + 1) // 2, weight_ticks, 0)
 
     def finish(m, _):
         rows = pl.ds(pl.multiple_of(m * mt, mt), mt)

time: 215 us -> 174 us (0.81)
  Pallas kernels: 210 us -> 170 us
    pallas_call x1, Pallas kernels: 210 us -> 170 us  [body(): pl.pallas_call(kernel, out_shape=[jax.ShapeDtypeStruct((units, feats), BF...]
where the time goes in v3:
time: 174 us
  Pallas kernels  170 us (98%)
  local copies, waits for them, and re-layouts  3.6 us (2%)
    pallas_call x1, Pallas kernels, body(): pl.pallas_call(kernel, out_shape=[jax.ShapeDtypeStruct((units, feats), BF...  170 us
    unnamed x4, local copies, waits for them, and re-layouts  3.6 us

profile of v3, /device:TPU:32, one launch (start us, length us, event | category | flops | bytes accessed | tf_op | source)
XLA Modules:
  0.0 174.1 jit_solution(7149848210866129154)
XLA Ops:
  0.6 169.8 %head.1 = (bf16[1024,1024]{1,0:T(8,128)(2,1)}, f32[1,128]{1,0:T(1,128)}) custom-call(bf16[128,1024]{1,0:T(8,128)(2,1)} %h_in.1, bf16[1024,1024]{1,0:T(8,128)(2,1)} %w_in.1, bf16[1024,4096]{1,0:T(8,128)(2,1)} %v_in.1, s32[1,128]{1,0:T(1,128)} %bitcast.2), custom_call_target="tpu_custom_call" | custom-call | tf_op jit(solution)/shard_map/head/pallas_call | solution.py:589
  170.5 0.0 copy-start
  170.5 3.1 %copy.8 = bf16[1024,1024]{1,0:T(8,128)(2,1)} copy(bf16[1024,1024]{1,0:T(8,128)(2,1)} %get-tuple-element.8) | data formatting | bytes 4194304
  173.6 0.0 copy-done
  173.6 0.5 copy.9
Async XLA Ops:
  170.5 3.1 %copy-start = (f32[1,128]{1,0:T(1,128)S(1)}, f32[1,128]{1,0:T(1,128)}, u32[]{:S(2)}) copy-start(f32[1,128]{1,0:T(1,128)} %get-tuple-element.5) | copy-start | bytes 1540

commit v4 on v3

--- a/solution.py
+++ b/solution.py
@@ -44,9 +44,9 @@
 
 def kernel(
     h_in, w_in, v_in, tgt, out, loss_out,
-    H, W, V, PT, S0, R, YS, YK, YR, YB, YC, TS, PRE, RES, D1, L, SL, RL, LYS, LYR, LF, G, LT, DR, DQ, DP,
+    H, W, V, PT, S0, R, YS, YK, YR, YB, YC, TS, TM, PRE, RES, D1, L, SL, RL, LYS, LYR, LF, G, LT, DR, DQ, DP,
     ACC, OUT,
-    loc, h_s, h_r, rs_s, rs_r, y_s, y_r, yc_r, t_s, t_r, l_s, l_r, ly_s, ly_r, g_s, g_r, lt_s, lt_r,
+    loc, h_s, h_r, rs_s, rs_r, y_s, y_r, yc_r, m_s, m_r, t_s, t_r, l_s, l_r, ly_s, ly_r, g_s, g_r, lt_s, lt_r,
     d_s, d_r, dy_s, dy_r, a_s, a_r, o_s,
 ):
     dp = lax.axis_index("dp")
@@ -71,7 +71,12 @@
     def out_target(slot):
         dx, a = offset_of(slot)
         there = ((x + dx) % 4) * 4 + ((y_lo + a) % 2) * 2 + (core + y_hi) % 2
-        return (there, dp)
+        return (there, shard)
+
+    def in_column(slot):
+        dx, a = offset_of(slot)
+        column = ((x + 4 - dx) % 4) * 4 + ((y_lo + a) % 2) * 2 + (core + y_hi) % 2
+        return (dp, column)
 
     flip = (core + shard % 2) % 2
 
@@ -215,16 +220,21 @@
                 R[d, r, k - 1, 0] = (mine(d) + R[d, r, k - 1, 0].astype(F32)).astype(BF16)
             send(R.at[d, r, k - 1, 0], R.at[d, r, k, 0], rs_s.at[3], rs_r.at[d, r, k], ring[d])
 
-    def hand_over(r):
-        device = out_target(r)
-
+    def move(src, dst, send_sem, recv_sem, device):
         @pl.when(is_self(device))
         def _():
-            pltpu.make_async_copy(TS.at[r], PRE.at[z], t_r).start()
+            pltpu.make_async_copy(src, dst, recv_sem).start()
 
         @pl.when(jnp.logical_not(is_self(device)))
         def _():
-            send(TS.at[r], PRE.at[z], t_s, t_r, device)
+            send(src, dst, send_sem, recv_sem, device)
+
+    def to_tokens(r):
+        move(TS.at[r], TM.at[r], m_s, m_r.at[r], out_target(r))
+
+    def to_features(r):
+        wait(TM.at[r], m_r.at[r])
+        move(TM.at[r], PRE.at[z], t_s, t_r, in_column(r))
 
     def pre_ticks(pair, _):
         for u in (0, 1):
@@ -233,6 +243,8 @@
                 @pl.when(live(t - PRE_LAG * s, ROUNDS))
                 def _(s=s, t=t, u=u):
                     (odd_step if (u - PRE_LAG * s) % 2 else even_step)(t - PRE_LAG * s, s)
+                    if s == 5:
+                        to_tokens(t - PRE_LAG * s)
 
             if u == 1:
                 @pl.when(t == 1)
@@ -255,19 +267,20 @@
 
             e = t - 5 * (PRE_LAG - 1)
 
-            @pl.when(jnp.logical_and(e >= 8, e <= 10))
+            @pl.when(jnp.logical_and(e >= 9, e <= 11))
             def _(e=e):
-                hand_over(2 * (e - 8))
-                hand_over(2 * (e - 8) + 1)
-
-            @pl.when(jnp.logical_and(e >= 11, e <= 12))
-            def _(e=e):
-                hand_over(e - 5)
+                to_features(2 * (e - 9))
+                to_features(2 * (e - 9) + 1)
+
+            @pl.when(e == 12)
+            def _():
+                to_features(6)
 
         return 0
 
     lax.fori_loop(0, (ROUNDS + 5 * PRE_LAG + 1) // 2, pre_ticks, 0)
 
+    to_features(7)
     wait(PRE, t_r)
     pre = PRE[...].reshape(128, units).astype(F32)
     RES[...] = (H[0].astype(F32) + pre / (1.0 + jnp.exp(-pre))).astype(BF16)
@@ -520,15 +533,14 @@
     wait(G.at[0, 0:4], g_s.at[1])
     wait(LT.at[0:7], lt_s)
 
-    @pl.when(own)
-    def _():
-        wait(DP.at[0, 0, 0:7], t_s)
-        wait(DP.at[0, 0, 0:7], d_s)
-
-    @pl.when(jnp.logical_not(own))
-    def _():
-        wait(eight, t_s)
-        wait(eight, d_s)
+    for sem, kept in ((m_s, y_hi == 0), (t_s, core == 0), (d_s, own)):
+        @pl.when(kept)
+        def _(sem=sem):
+            wait(DP.at[0, 0, 0:7], sem)
+
+        @pl.when(jnp.logical_not(kept))
+        def _(sem=sem):
+            wait(eight, sem)
 
     pltpu.make_async_copy(OUT, out, o_s).wait()
 
@@ -554,6 +566,7 @@
         vmem((pairs, RING, 16, units), BF16),
         vmem((pairs, RING, 16, units), BF16),
         vmem((ROUNDS, 16, units), BF16),
+        vmem((ROUNDS, 16, units), BF16),
         vmem((8, 16, units), BF16),
         vmem((128, units), BF16),
         vmem((128, units), F32),
@@ -574,6 +587,7 @@
         one, dma((2 * ROUNDS,)),
         dma((4,)), dma((2, ROUNDS, 4)),
         dma((2,)), dma((pairs,)), dma((pairs, 5)),
+        one, dma((ROUNDS,)),
         one, one,
         dma((2,)), dma((2, PARTS, 4)),
         one, dma((PARTS,)),

time: 174 us -> 164 us (0.943); the launches traced: 174 us -> 162 us
  Pallas kernels: 170 us -> 158 us
    pallas_call x1, Pallas kernels: 170 us -> 158 us  [body(): pl.pallas_call(kernel, out_shape=[jax.ShapeDtypeStruct((units, feats), BF...]
where the time goes in v4:
time: 164 us; the launch traced here: 162 us
  Pallas kernels  158 us (96%)
  local copies, waits for them, and re-layouts  3.6 us (2%)
    pallas_call x1, Pallas kernels, body(): pl.pallas_call(kernel, out_shape=[jax.ShapeDtypeStruct((units, feats), BF...  158 us
    unnamed x4, local copies, waits for them, and re-layouts  3.6 us

profile of v4, /device:TPU:32, one launch (start us, length us, event | category | flops | bytes accessed | tf_op | source)
XLA Modules:
  0.0 162.1 jit_solution(12028164425869146690)
XLA Ops:
  0.6 157.9 %head.1 = (bf16[1024,1024]{1,0:T(8,128)(2,1)}, f32[1,128]{1,0:T(1,128)}) custom-call(bf16[128,1024]{1,0:T(8,128)(2,1)} %h_in.1, bf16[1024,1024]{1,0:T(8,128)(2,1)} %w_in.1, bf16[1024,4096]{1,0:T(8,128)(2,1)} %v_in.1, s32[1,128]{1,0:T(1,128)} %bitcast.2), custom_call_target="tpu_custom_call" | custom-call | tf_op jit(solution)/shard_map/head/pallas_call | solution.py:603
  158.5 0.0 copy-start
  158.5 3.1 %copy.8 = bf16[1024,1024]{1,0:T(8,128)(2,1)} copy(bf16[1024,1024]{1,0:T(8,128)(2,1)} %get-tuple-element.8) | data formatting | bytes 4194304
  161.6 0.0 copy-done
  161.6 0.5 copy.9
Async XLA Ops:
  158.5 3.1 %copy-start = (f32[1,128]{1,0:T(1,128)S(1)}, f32[1,128]{1,0:T(1,128)}, u32[]{:S(2)}) copy-start(f32[1,128]{1,0:T(1,128)} %get-tuple-element.5) | copy-start | bytes 1540

commit v5 on v4

--- a/solution.py
+++ b/solution.py
@@ -45,9 +45,9 @@
 def kernel(
     h_in, w_in, v_in, tgt, out, loss_out,
     H, W, V, PT, S0, R, YS, YK, YR, YB, YC, TS, TM, PRE, RES, D1, L, SL, RL, LYS, LYR, LF, G, LT, DR, DQ, DP,
-    ACC, OUT,
+    ACC,
     loc, h_s, h_r, rs_s, rs_r, y_s, y_r, yc_r, m_s, m_r, t_s, t_r, l_s, l_r, ly_s, ly_r, g_s, g_r, lt_s, lt_r,
-    d_s, d_r, dy_s, dy_r, a_s, a_r, o_s,
+    d_s, d_r, dy_s, dy_r, a_s, a_r,
 ):
     dp = lax.axis_index("dp")
     shard = lax.axis_index("shard")
@@ -396,6 +396,11 @@
             )
             DR[...] = jnp.where(p == 0, part, DR[...] + part)
 
+        for k in (1, 2, 3, 4):
+            @pl.when(t == GRAD_LAG * k)
+            def _(k=k):
+                loss_step(k)
+
         return 0
 
     DR[...] = jnp.zeros_like(DR)
@@ -415,8 +420,6 @@
         def _(g=g, place=place, device=device):
             send(DQ.at[g], place, d_s, d_r.at[slot], device)
 
-    for k in range(1, 5):
-        loss_step(k)
     column = jnp.sum(LT[...].reshape(128, 128).astype(F32), axis=1, keepdims=True)
     diagonal = lax.broadcasted_iota(jnp.int32, (128, 128), 0) == lax.broadcasted_iota(jnp.int32, (128, 128), 1)
     loss_out[...] = jnp.sum(jnp.where(diagonal, column, 0.0), axis=0, keepdims=True)
@@ -505,8 +508,7 @@
 
     def finish(m, _):
         rows = pl.ds(pl.multiple_of(m * mt, mt), mt)
-        OUT[rows, :] = (ACC[rows, :] + outer(ROUNDS - 1, m)).astype(BF16)
-        pltpu.make_async_copy(OUT.at[rows], out.at[rows], o_s).start()
+        out[rows, :] = (ACC[rows, :] + outer(ROUNDS - 1, m)).astype(BF16)
         return 0
 
     lax.fori_loop(0, units // mt, finish, 0)
@@ -541,8 +543,6 @@
         @pl.when(jnp.logical_not(kept))
         def _(sem=sem):
             wait(eight, sem)
-
-    pltpu.make_async_copy(OUT, out, o_s).wait()
 
 
 def body(hidden, head_weight, vocab_head, targets):
@@ -582,7 +582,6 @@
         vmem((8, 16, units), BF16),
         vmem((ROUNDS, 2, RING, 16, units), BF16),
         vmem((units, feats), F32),
-        vmem((units, feats), BF16),
         dma((3,)),
         one, dma((2 * ROUNDS,)),
         dma((4,)), dma((2, ROUNDS, 4)),
@@ -596,21 +595,20 @@
         one, dma((ROUNDS,)),
         dma((2,)), dma((ROUNDS,)),
         dma((4,)), dma((2, ROUNDS, 4)),
-        one,
     ]
     anywhere = pl.BlockSpec(memory_space=pl.ANY)
     inside = pl.BlockSpec(memory_space=pltpu.VMEM)
     grad, loss = pl.pallas_call(
         kernel,
         out_shape=[
-            jax.ShapeDtypeStruct((units, feats), BF16),
+            pltpu.VMEM((units, feats), BF16),
             jax.ShapeDtypeStruct((1, 128), F32),
         ],
         in_specs=[anywhere, anywhere, anywhere, inside],
-        out_specs=[anywhere, inside],
+        out_specs=[inside, inside],
         scratch_shapes=scratch,
         compiler_params=pltpu.CompilerParams(
-            collective_id=0, has_side_effects=True, vmem_limit_bytes=58 * 1024 * 1024
+            collective_id=0, has_side_effects=True, vmem_limit_bytes=56 * 1024 * 1024
         ),
         name="head",
     )(hidden, head_weight, vocab_head, targets.reshape(1, 128))

time: 164 us -> 160 us (0.976)
  the two profiles are of different devices: /device:TPU:32 before, /device:TPU:1 now
where the time goes in v5:
time: 160 us
  Pallas kernels  157 us (98%)
  local copies, waits for them, and re-layouts  1.84 us (1%)
    pallas_call x1, Pallas kernels, body(): pl.pallas_call(kernel, out_shape=[pltpu.VMEM((units, feats), BF16), jax.S...  157 us

profile of v5, /device:TPU:1, one launch (start us, length us, event | category | flops | bytes accessed | tf_op | source)
XLA Modules:
  0.0 159.9 jit_solution(2238600789689467325)
XLA Ops:
  0.6 157.4 %head.1 = (bf16[1024,1024]{1,0:T(8,128)(2,1)S(1)}, f32[1,128]{1,0:T(1,128)}) custom-call(bf16[128,1024]{1,0:T(8,128)(2,1)} %h_in.1, bf16[1024,1024]{1,0:T(8,128)(2,1)} %w_in.1, bf16[1024,4096]{1,0:T(8,128)(2,1)} %v_in.1, s32[1,128]{1,0:T(1,128)} %bitcast.2), custom_call_target="tpu_custom_call" | custom-call | tf_op jit(solution)/shard_map/head/pallas_call | solution.py:601
  158.0 0.0 copy-start
  158.0 1.3 copy.8
  159.3 0.0 copy-done
  159.3 0.5 copy.9
Async XLA Ops:
  158.0 1.3 copy-start

commit v6 on v5

--- a/solution.py
+++ b/solution.py
@@ -149,6 +149,18 @@
             return 0
 
         lax.fori_loop(0, units // nt, tile, 0)
+
+    def first_product(b):
+        def tile(n, _):
+            cols = pl.ds(pl.multiple_of(n * nt, nt), nt)
+            PT[0, b, :, :, cols] = jnp.dot(
+                H[b], W[:, cols], preferred_element_type=F32
+            ).reshape(RING, 16, nt)
+            return 0
+
+        lax.fori_loop(0, units // nt, tile, 0)
+
+    first_product(0)
 
     def even_step(r, s):
         q = r // 2
@@ -254,7 +266,17 @@
             @pl.when(t < ROUNDS)
             def _(t=t, u=u):
                 wait(H.at[2 * t + 1], h_r.at[2 * t + 1])
-                product(t)
+                if u:
+                    product(t)
+                else:
+                    @pl.when(t == 0)
+                    def _():
+                        first_product(1)
+
+                    @pl.when(t > 0)
+                    def _():
+                        product(t)
+
                 (odd_step if u else even_step)(t, 0)
 
             @pl.when(jnp.logical_and(t >= 1, t < ROUNDS - 1))

time: 160 us -> 160 us (level)
  no operation moved by 1% of the time
where the time goes in v6:
time: 160 us
  Pallas kernels  157 us (98%)
  local copies, waits for them, and re-layouts  1.84 us (1%)
    pallas_call x1, Pallas kernels, body(): pl.pallas_call(kernel, out_shape=[pltpu.VMEM((units, feats), BF16), jax.S...  157 us

profile of v6, /device:TPU:1, one launch (start us, length us, event | category | flops | bytes accessed | tf_op | source)
XLA Modules:
  0.0 159.9 jit_solution(13768216667730687241)
XLA Ops:
  0.6 157.4 %head.1 = (bf16[1024,1024]{1,0:T(8,128)(2,1)S(1)}, f32[1,128]{1,0:T(1,128)}) custom-call(bf16[128,1024]{1,0:T(8,128)(2,1)} %h_in.1, bf16[1024,1024]{1,0:T(8,128)(2,1)} %w_in.1, bf16[1024,4096]{1,0:T(8,128)(2,1)} %v_in.1, s32[1,128]{1,0:T(1,128)} %bitcast.2), custom_call_target="tpu_custom_call" | custom-call | tf_op jit(solution)/shard_map/head/pallas_call | solution.py:623
  158.1 0.0 copy-start
  158.1 1.3 copy.8
  159.4 0.0 copy-done
  159.4 0.5 copy.9
Async XLA Ops:
  158.1 1.3 copy-start
